TPU v7x, 32 devices: a whole 2x2x4 slice. The times are simulated.
32 devices in a mesh: groups: 2 (over x), goal: 16 (over z, y, core).
Axes of the slice: x: 2, y: 2, z: 4, core: 2. Of those that a mesh axis runs over, the one named last changes fastest.
Arguments:
- queries: bfloat16 [128, 64, 4096], P(('groups', 'goal')), parts along dimension 0, may hold values from -8 to 8
- goal_keys: bfloat16 [32, 256, 4096], P(('groups', 'goal')), parts along dimension 0, may hold values from -8 to 8
- goal_values: bfloat16 [32, 256, 4096], P(('groups', 'goal')), parts along dimension 0, may hold values from -6 to 6
- out_weight: bfloat16 [4096, 2048], P('goal'), may hold values from -0.5 to 0.5
- tactic_goal: int32 [128, 1], P(('groups', 'goal')), parts along dimension 0, may hold values from 0 to 15
- tactic_len: int32 [128], P(('groups', 'goal')), parts along dimension 0, may hold values from 1 to 64
Outputs:
- projected: bfloat16 [128, 64, 2048], P(('groups', 'goal')), parts along dimension 0
There are 2 independent parts, one for each index of `groups`. A program takes and returns all parts, laid end to end along the dimension named above; an argument that names none is the same for every part. Nothing has to cross between parts.
Inputs may be any that keep to these rules, and one draw needn't show every extreme that they name: `tactic_goal`: every goal is read by at least one tactic; tactics per goal are uneven. `tactic_len`: the live positions of a tactic are its leading ones.
All inputs are finite; a program needn't handle non-finite values.
Results may differ from a plain program's by a relative error of at most 0.01.
Values may be sent and summed in bfloat16 or wider, within the bound.
A program may use at most 192 MiB of HBM per device.

v0:
```python
import math
import jax
import jax.numpy as jnp
from jax import lax
from jax.sharding import PartitionSpec as P

DH = 64


def attend_block(query_block, keys_heads, values_heads, block_ids):
    tact_count = query_block.shape[0]
    row_count = query_block.shape[1]
    width_local = query_block.shape[2]
    head_count = width_local // DH
    keys_tact = jnp.take(keys_heads, block_ids, axis=0).reshape(tact_count, -1, head_count, DH)
    vals_tact = jnp.take(values_heads, block_ids, axis=0).reshape(tact_count, -1, head_count, DH)
    query_four = query_block.reshape(tact_count, row_count, head_count, DH)
    scores = jnp.einsum(
        "tihd,tjhd->thij", query_four, keys_tact, preferred_element_type=jnp.float32
    )
    biggest = jnp.max(scores, axis=-1, keepdims=True)
    powers = jnp.exp(scores - biggest)
    weights = (powers / jnp.sum(powers, axis=-1, keepdims=True)).astype(jnp.bfloat16)
    attended = jnp.einsum("thij,tjhd->tihd", weights, vals_tact, preferred_element_type=jnp.float32)
    return attended.reshape(tact_count, row_count, width_local).astype(jnp.bfloat16)


def attend(query_piece, keys_heads, values_heads, goal_ids):
    tact_count = query_piece.shape[0]
    row_count = query_piece.shape[1]
    width_local = query_piece.shape[2]
    block_size = math.gcd(tact_count, 64)
    block_count = tact_count // block_size
    query_blocks = query_piece.reshape(block_count, block_size, row_count, width_local)
    id_blocks = goal_ids.reshape(block_count, block_size)

    def one_block(operands):
        return attend_block(operands[0], keys_heads, values_heads, operands[1])

    results = lax.map(one_block, (query_blocks, id_blocks))
    return results.reshape(tact_count, row_count, width_local)


def shards(queries, goal_keys, goal_values, out_weight, tactic_goal, tactic_len):
    goal_ids = lax.all_gather(tactic_goal[:, 0], "goal", axis=0, tiled=True)
    keys_heads, values_heads = (
        lax.all_to_all(goal_keys, "goal", split_axis=2, concat_axis=0, tiled=True),
        lax.all_to_all(goal_values, "goal", split_axis=2, concat_axis=0, tiled=True),
    )
    query_heads = lax.all_to_all(queries, "goal", split_axis=2, concat_axis=0, tiled=True)
    attended = attend(query_heads, keys_heads, values_heads, goal_ids)
    merged = lax.all_to_all(attended, "goal", split_axis=0, concat_axis=2, tiled=True)
    live_rows = jnp.arange(merged.shape[1])[None, :] < tactic_len[:, None]
    context = jnp.where(live_rows[:, :, None], merged, jnp.zeros_like(merged))
    tact_local = context.shape[0]
    row_count = context.shape[1]
    flat = context.reshape(tact_local * row_count, context.shape[2])
    projected = jnp.dot(
        flat,
        lax.all_gather(out_weight, "goal", axis=0, tiled=True),
        preferred_element_type=jnp.float32,
    )
    return projected.astype(jnp.bfloat16).reshape(tact_local, row_count, out_weight.shape[1])


def solution(mesh):
    return jax.shard_map(
        shards,
        mesh=mesh,
        in_specs=(
            P(("groups", "goal"), None, None),
            P(("groups", "goal"), None, None),
            P(("groups", "goal"), None, None),
            P("goal", None),
            P(("groups", "goal"), None),
            P(("groups", "goal")),
        ),
        out_specs=P(("groups", "goal"), None, None),
        check_vma=False,
    )
```

profile of v0, /device:TPU:13, one launch (start us, length us, event | category | flops | bytes accessed | tf_op | source)
XLA Modules:
  0.0 509.1 jit_solution(2314349538631211243)
XLA Ops:
  7.3 10.1 %copy.23 = bf16[1,256,4096]{1,0,2:T(2,128)(2,1)} copy(bf16[1,256,4096]{2,1,0:T(8,128)(2,1)} %param.10) | data formatting | bytes 4194304 | tf_op args[2]
  17.8 21.7 %reduce.1 = bf16[4096,256]{1,0:T(8,128)(2,1)S(1)} reduce(bf16[4096,1,256]{2,1,0:T(2,128)(2,1)} %bitcast.58, bf16[]{:T(256)} %broadcast.32), dimensions={1}, to_apply=%bitcast.44.reduce_sub_computation | reduce | bytes 4194306
  41.6 6.6 %all-to-all-start = ((bf16[16,2,32768]{2,1,0:T(2,128)(2,1)}), bf16[16,2,32768]{2,1,0:T(2,128)(2,1)S(1)}, u32[]{:S(2)}, u32[]{:S(2)}) async-start(bf16[16,2,32768]{2,1,0:T(2,128)(2,1)} %reshape.91), calls=%async_computation | async-start | bytes 4194304 | tf_op jit(solution)/shard_map/all_to_all | solution.py:48
  48.1 10.1 %copy.26 = bf16[1,256,4096]{1,0,2:T(2,128)(2,1)} copy(bf16[1,256,4096]{2,1,0:T(8,128)(2,1)} %param.9) | data formatting | bytes 4194304 | tf_op args[1]
  58.2 23.0 %reduce = bf16[4096,256]{1,0:T(8,128)(2,1)} reduce(bf16[4096,1,256]{2,1,0:T(2,128)(2,1)} %bitcast.59, bf16[]{:T(256)} %broadcast.32), dimensions={1}, to_apply=%bitcast.46.reduce_sub_computation | reduce | bytes 4194306
  85.1 58.2 %all-to-all-done = bf16[16,2,32768]{2,1,0:T(2,128)(2,1)S(1)} async-done(((bf16[16,2,32768]{2,1,0:T(2,128)(2,1)}), bf16[16,2,32768]{2,1,0:T(2,128)(2,1)S(1)}, u32[]{:S(2)}, u32[]{:S(2)}) %all-to-all-start) | async-done | bytes 2097184 | tf_op jit(solution)/shard_map/all_to_all | solution.py:48
  147.7 7.0 %copy.29 = bf16[4,64,4096]{1,0,2:T(4,128)(2,1)} copy(bf16[4,64,4096]{2,1,0:T(8,128)(2,1)} %param.8) | data formatting | bytes 4194304 | tf_op args[0]
  154.7 7.5 %reshape.95 = bf16[16,2,32768]{2,1,0:T(2,128)(2,1)} reshape(bf16[4096,4,64]{2,1,0:T(4,128)(2,1)} %bitcast.63) | data formatting | bytes 4194304
  162.3 52.0 %all-to-all-done.1 = bf16[16,2,32768]{2,1,0:T(2,128)(2,1)} async-done(((bf16[16,2,32768]{2,1,0:T(2,128)(2,1)}), bf16[16,2,32768]{2,1,0:T(2,128)(2,1)}, u32[]{:S(2)}, u32[]{:S(2)}) %all-to-all-start.1) | async-done | bytes 2097184 | tf_op jit(solution)/shard_map/all_to_all | solution.py:47
  220.4 44.1 %all-reduce = s32[64]{0:T(128)S(1)} all-reduce(s32[64]{0:T(128)S(1)} %bitcast_dynamic-update-slice_fusion), channel_id=2, replica_groups=mesh['groups'=2,'goal'=16] {'goal'}, use_global_device_ids=true, to_apply=%add | all-reduce | flops 64 | bytes 512 | tf_op jit(solution)/shard_map/all_gather | solution.py:45
  264.5 6.8 %reshape.92 = bf16[4096,1,256]{2,1,0:T(2,128)(2,1)} reshape(bf16[16,2,32768]{2,1,0:T(2,128)(2,1)S(1)} %all-to-all-done) | data formatting | bytes 4194304
  278.0 10.5 %reshape.94 = bf16[4096,1,256]{2,1,0:T(2,128)(2,1)} reshape(bf16[16,2,32768]{2,1,0:T(2,128)(2,1)} %all-to-all-done.1) | data formatting | bytes 4194304
  296.3 5.5 %gather_fusion = bf16[64,256,256]{2,1,0:T(8,128)(2,1)} fusion(bf16[16,256,256]{2,1,0:T(8,128)(2,1)S(1)} %bitcast.56, s32[1024]{0:T(1024)S(1)} %pad_clamp_fusion), kind=kCustom, calls=%fused_computation.clone | custom fusion | bytes 16777472 | tf_op jit(solution)/shard_map/while/body/eval_jaxpr/jit(_take)/gather | solution.py:16
  301.8 7.1 %gather_fusion.1 = bf16[64,256,256]{2,1,0:T(8,128)(2,1)} fusion(bf16[16,256,256]{2,1,0:T(8,128)(2,1)} %bitcast.57, s32[1024]{0:T(1024)S(1)} %pad_clamp_fusion), kind=kCustom, calls=%fused_computation.1.clone | custom fusion | bytes 16777472 | tf_op jit(solution)/shard_map/while/body/eval_jaxpr/jit(_take)/gather | solution.py:15
  308.9 11.6 %broadcast_select_fusion = (bf16[64,256,256]{2,1,0:T(8,128)(2,1)}, bf16[64,256,256]{2,1,0:T(8,128)(2,1)}) fusion(bf16[64,256,256]{2,1,0:T(8,128)(2,1)} %gather_fusion.1, pred[64]{0:T(512)(128)(4,1)S(1)} %compare_and_fusion, bf16[64,256,256]{2,1,0:T(8,128)(2,1)} %gather_fusion), kind=kLoop, calls=%fused_computation.9 | loop fusion | flops 8388608 | bytes 33554496 | tf_op jit(solution)/shard_map/while/body/eval_jaxpr/jit(_take)/select_n | solution.py:15
  320.5 11.9 %copy.28 = bf16[64,256,256]{1,2,0:T(8,128)(2,1)} copy(bf16[64,256,256]{2,1,0:T(8,128)(2,1)} %get-tuple-element.16) | data formatting | bytes 16777216 | tf_op jit(solution)/shard_map/while/body/eval_jaxpr/jit(_take)/select_n | solution.py:15
  332.4 7.5 %reshape.96 = bf16[4096,4,64]{2,1,0:T(4,128)(2,1)} reshape(bf16[16,2,32768]{2,1,0:T(2,128)(2,1)} %all-to-all-done.2) | data formatting | bytes 4194304
  348.5 11.9 %copy.25 = bf16[64,256,256]{1,2,0:T(8,128)(2,1)} copy(bf16[64,256,256]{2,1,0:T(8,128)(2,1)} %get-tuple-element.17) | data formatting | bytes 16777216 | tf_op jit(solution)/shard_map/while/body/eval_jaxpr/jit(_take)/select_n | solution.py:16
  360.4 12.7 %fusion.6 = f32[64,4,256,64]{2,3,1,0:T(8,128)} fusion(bf16[64,256,4,64]{1,3,2,0:T(8,128)(2,1)} %bitcast.55, bf16[64,64,4,64]{3,2,1,0:T(4,128)(2,1)} %reshape.60), kind=kOutput, calls=%fused_computation.11 | convolution fusion | flops 536870912 | bytes 27262976 | tf_op jit(solution)/shard_map/while/body/eval_jaxpr/tihd,tjhd->thij/dot_general | solution.py:18
  373.1 14.6 %fusion.18 = f32[64,4,64]{2,1,0:T(4,128)S(1)} fusion(f32[64,4,256,64]{2,3,1,0:T(8,128)} %fusion.6), kind=kOutput, calls=%fused_computation.25 | output fusion | flops 8388863 | bytes 16842752 | tf_op jit(solution)/shard_map/while/body/eval_jaxpr/sub | solution.py:22
  387.7 43.3 %fusion.8 = bf16[64,4,64,64]{3,2,1,0:T(8,128)(2,1)} fusion(bf16[64,256,4,64]{1,3,2,0:T(8,128)(2,1)} %bitcast.67, f32[64,4,64]{2,1,0:T(4,128)S(1)} %fusion.18, f32[64,4,256,64]{2,3,1,0:T(8,128)} %fusion.6), kind=kOutput, calls=%fused_computation.13 | convolution fusion | flops 550519040 | bytes 27328512 | tf_op jit(solution)/shard_map/while/body/eval_jaxpr/thij,tjhd->tihd/dot_general | solution.py:24
  435.9 7.5 %all-to-all-start.3 = ((bf16[64,64,256]{2,1,0:T(8,128)(2,1)}), bf16[64,64,256]{2,1,0:T(8,128)(2,1)S(1)}, u32[]{:S(2)}, u32[]{:S(2)}) async-start(bf16[64,64,256]{2,1,0:T(8,128)(2,1)} %copy.32), calls=%async_computation.3 | async-start | bytes 4194304 | tf_op jit(solution)/shard_map/all_to_all | solution.py:52
  443.6 47.3 %all-to-all-done.3 = bf16[64,64,256]{2,1,0:T(8,128)(2,1)S(1)} async-done(((bf16[64,64,256]{2,1,0:T(8,128)(2,1)}), bf16[64,64,256]{2,1,0:T(8,128)(2,1)S(1)}, u32[]{:S(2)}, u32[]{:S(2)}) %all-to-all-start.3) | async-done | bytes 2097184 | tf_op jit(solution)/shard_map/all_to_all | solution.py:52
  493.0 9.3 %convolution_convert_fusion = bf16[256,2048]{1,0:T(8,128)(2,1)} fusion(bf16[4096,2048]{1,0:T(8,128)(2,1)} %all-gather.3.cloned.1.call-done, bf16[256,4096]{1,0:T(8,128)(2,1)S(1)} %bitcast.71, pred[256]{0:T(512)(128)(4,1)S(1)} %lt.30), kind=kOutput, calls=%fused_computation.14 | convolution fusion | flops 4296540160 | bytes 19923200 | tf_op jit(solution)/shard_map/dot_general | solution.py:58
  (32 shorter events, 47.3 us)
Async XLA Ops:
  6.5 486.4 %all-gather.3.cloned.1.call-start = ((), (), s32[]{:S(2)}) async-start(), calls=%async_computation.4 | async-start | bytes 17825792 | tf_op jit(solution)/shard_map/all_gather | solution.py:60
  41.6 101.8 %all-to-all-start = ((bf16[16,2,32768]{2,1,0:T(2,128)(2,1)}), bf16[16,2,32768]{2,1,0:T(2,128)(2,1)S(1)}, u32[]{:S(2)}, u32[]{:S(2)}) async-start(bf16[16,2,32768]{2,1,0:T(2,128)(2,1)} %reshape.91), calls=%async_computation | async-start | bytes 4194304 | tf_op jit(solution)/shard_map/all_to_all | solution.py:48
  143.3 71.0 %all-to-all-start.1 = ((bf16[16,2,32768]{2,1,0:T(2,128)(2,1)}), bf16[16,2,32768]{2,1,0:T(2,128)(2,1)}, u32[]{:S(2)}, u32[]{:S(2)}) async-start(bf16[16,2,32768]{2,1,0:T(2,128)(2,1)} %reshape.93), calls=%async_computation.1 | async-start | bytes 4194304 | tf_op jit(solution)/shard_map/all_to_all | solution.py:47
  147.7 71.4 %copy-start.2 = (u32[32]{0:T(128)S(1)}, u32[32]{0:T(128)}, u32[]{:S(2)}) copy-start(u32[32]{0:T(128)} %constant.37) | copy-start | bytes 388
  147.7 72.6 %copy-start = (s32[4,1]{0,1:T(1,128)S(1)}, s32[4,1]{0,1:T(1,128)}, u32[]{:S(2)}) copy-start(s32[4,1]{0,1:T(1,128)} %param.12) | copy-start | bytes 52
  214.3 118.2 %all-to-all-start.2 = ((bf16[16,2,32768]{2,1,0:T(2,128)(2,1)}), bf16[16,2,32768]{2,1,0:T(2,128)(2,1)}, u32[]{:S(2)}, u32[]{:S(2)}) async-start(bf16[16,2,32768]{2,1,0:T(2,128)(2,1)} %reshape.95), calls=%async_computation.2 | async-start | bytes 4194304 | tf_op jit(solution)/shard_map/all_to_all | solution.py:50
  431.1 12.3 %copy-start.1 = (s32[4]{0:T(128)S(1)}, s32[4]{0:T(128)}, u32[]{:S(2)}) copy-start(s32[4]{0:T(128)} %param.13) | copy-start | bytes 52
  435.9 54.9 %all-to-all-start.3 = ((bf16[64,64,256]{2,1,0:T(8,128)(2,1)}), bf16[64,64,256]{2,1,0:T(8,128)(2,1)S(1)}, u32[]{:S(2)}, u32[]{:S(2)}) async-start(bf16[64,64,256]{2,1,0:T(8,128)(2,1)} %copy.32), calls=%async_computation.3 | async-start | bytes 4194304 | tf_op jit(solution)/shard_map/all_to_all | solution.py:52
Sparse Core Ops, SparseCore 0:
  9.5 193.1 all-gather.2
where the time goes:
time: 512 us; the launch traced here: 509 us
  waiting for transfers between devices  158 us (31%)
  local copies, waits for them, and re-layouts  133 us (26%)
  other arithmetic  70.9 us (14%)
  matrix products  65.3 us (13%)
  blocking collectives  44.1 us (9%)
  starting transfers between devices  23.2 us (5%)
  between operations  14.2 us (3%)
    unnamed x22, local copies, waits for them, and re-layouts  75.4 us
    all_to_all x1, waiting for transfers between devices, shards(): lax.all_to_all(goal_values, 'goal', split_axis=2, concat_axis=0, tiled=True)  58.2 us
    all_to_all x1, waiting for transfers between devices, shards(): lax.all_to_all(goal_keys, 'goal', split_axis=2, concat_axis=0, tiled=True)  52 us
    all_to_all x1, waiting for transfers between devices, shards(): lax.all_to_all(attended, 'goal', split_axis=0, concat_axis=2, tiled=True)  47.3 us
    unnamed x2, other arithmetic  44.6 us
    all_gather x1, blocking collectives, shards(): goal_ids = lax.all_gather(tactic_goal[:, 0], 'goal', axis=0, tiled=True)  44.1 us
    dot_general x1, matrix products, attend_block(): jnp.einsum('thij,tjhd->tihd', weights, vals_tact, preferred_element_type=...  43.3 us
    sub x1, other arithmetic, attend_block(): powers = jnp.exp(scores - biggest)  14.6 us
  transfers between devices with their start and end apart: 5, of which 3 were waited for; matrix products, arithmetic and copies ran while one was open for 51% of the time, Pallas kernels for 0%

commit v1 on v0

--- a/solution.py
+++ b/solution.py
@@ -5,6 +5,18 @@
 from jax.sharding import PartitionSpec as P
 
 DH = 64
+
+
+def sent_to_each(x, axis, split, join):
+    ways, here = (lax.axis_size(axis), lax.axis_index(axis))
+    width = x.shape[split] // ways
+    turned = jnp.roll(x, -here * width, axis=split)
+    got = [lax.slice_in_dim(turned, 0, width, axis=split)]
+    for far in range(1, ways):
+        sent = lax.slice_in_dim(turned, far * width, (far + 1) * width, axis=split)
+        got.append(lax.ppermute(sent, axis, [(d, (d + far) % ways) for d in range(ways)]))
+    line = jnp.concatenate(got[::-1], axis=join)
+    return jnp.roll(line, (here + 1) * got[0].shape[join], axis=join)
 
 
 def attend_block(query_block, keys_heads, values_heads, block_ids):
@@ -44,7 +56,7 @@
 def shards(queries, goal_keys, goal_values, out_weight, tactic_goal, tactic_len):
     goal_ids = lax.all_gather(tactic_goal[:, 0], "goal", axis=0, tiled=True)
     keys_heads, values_heads = (
-        lax.all_to_all(goal_keys, "goal", split_axis=2, concat_axis=0, tiled=True),
+        sent_to_each(goal_keys, "goal", 2, 0),
         lax.all_to_all(goal_values, "goal", split_axis=2, concat_axis=0, tiled=True),
     )
     query_heads = lax.all_to_all(queries, "goal", split_axis=2, concat_axis=0, tiled=True)

time: 512 us -> 490 us (0.957)
  waiting for transfers between devices: 158 us -> 55.7 us
  starting transfers between devices: 23.2 us -> 81.2 us
  blocking collectives: 44.1 us -> 87.6 us
  other arithmetic: 70.9 us -> 50.5 us
    all_to_all x1, waiting for transfers between devices: 58.2 us -> 0.01 us  [shards(): lax.all_to_all(goal_values, 'goal', split_axis=2, concat_axis=0, tiled=True)]
    ppermute x0 -> x15, starting transfers between devices: none -> 55.8 us  [sent_to_each(): lax.ppermute(sent, axis, [(d, (d + far) % ways) for d in range(ways)])]
    all_to_all x1 -> x0, waiting for transfers between devices: 52 us -> none  [shards(): lax.all_to_all(goal_keys, 'goal', split_axis=2, concat_axis=0, tiled=True)]
    all_gather x1, blocking collectives: 44.1 us -> 87.6 us  [shards(): goal_ids = lax.all_gather(tactic_goal[:, 0], 'goal', axis=0, tiled=True)]
    unnamed x2 -> x1, other arithmetic: 44.6 us -> 21.7 us
    all_to_all x1, starting transfers between devices: 4.75 us -> 12.7 us  [shards(): lax.all_to_all(queries, 'goal', split_axis=2, concat_axis=0, tiled=True)]
    ppermute x0 -> x15, waiting for transfers between devices: none -> 7.69 us  [sent_to_each(): lax.ppermute(sent, axis, [(d, (d + far) % ways) for d in range(ways)])]
    unnamed x22 -> x57, local copies, waits for them, and re-layouts: 75.4 us -> 77.3 us
  transfers between devices with their start and end apart: 5 -> 19, of which waited for: 3 -> 7; matrix products, arithmetic and copies ran while one was open for 51% -> 49% of each run, Pallas kernels for 0% -> 0%
where the time goes in v1:
time: 490 us; the launch traced here: 488 us
  local copies, waits for them, and re-layouts  133 us (27%)
  blocking collectives  87.6 us (18%)
  starting transfers between devices  81.2 us (17%)
  matrix products  65.4 us (13%)
  waiting for transfers between devices  55.7 us (11%)
  other arithmetic  50.5 us (10%)
  between operations  14.1 us (3%)
    all_gather x1, blocking collectives, shards(): goal_ids = lax.all_gather(tactic_goal[:, 0], 'goal', axis=0, tiled=True)  87.6 us
    unnamed x57, local copies, waits for them, and re-layouts  77.3 us
    ppermute x15, starting transfers between devices, sent_to_each(): lax.ppermute(sent, axis, [(d, (d + far) % ways) for d in range(ways)])  55.8 us
    all_to_all x1, waiting for transfers between devices, shards(): lax.all_to_all(attended, 'goal', split_axis=0, concat_axis=2, tiled=True)  47.3 us
    dot_general x1, matrix products, attend_block(): jnp.einsum('thij,tjhd->tihd', weights, vals_tact, preferred_element_type=...  43.3 us
    unnamed x1, other arithmetic  21.7 us
    sub x1, other arithmetic, attend_block(): powers = jnp.exp(scores - biggest)  14.8 us
    dot_general x1, matrix products, attend_block(): jnp.einsum('tihd,tjhd->thij', query_four, keys_tact, preferred_element_ty...  12.7 us
  transfers between devices with their start and end apart: 19, of which 7 were waited for; matrix products, arithmetic and copies ran while one was open for 49% of the time, Pallas kernels for 0%

profile of v1, /device:TPU:13, one launch (start us, length us, event | category | flops | bytes accessed | tf_op | source)
XLA Modules:
  0.0 487.6 jit_solution(9663848386074978342)
XLA Ops:
  7.3 10.0 %copy.20 = bf16[1,256,4096]{1,0,2:T(2,128)(2,1)} copy(bf16[1,256,4096]{2,1,0:T(8,128)(2,1)} %param.10) | data formatting | bytes 4194304 | tf_op args[2]
  17.8 21.7 %reduce = bf16[4096,256]{1,0:T(8,128)(2,1)S(1)} reduce(bf16[4096,1,256]{2,1,0:T(2,128)(2,1)} %bitcast.51, bf16[]{:T(256)} %broadcast.34), dimensions={1}, to_apply=%bitcast.40.reduce_sub_computation | reduce | bytes 4194306
  41.5 6.6 %all-to-all-start = ((bf16[16,2,32768]{2,1,0:T(2,128)(2,1)}), bf16[16,2,32768]{2,1,0:T(2,128)(2,1)}, u32[]{:S(2)}, u32[]{:S(2)}) async-start(bf16[16,2,32768]{2,1,0:T(2,128)(2,1)} %reshape.91), calls=%async_computation | async-start | bytes 4194304 | tf_op jit(solution)/shard_map/all_to_all | solution.py:60
  58.3 87.6 %all-reduce = s32[64]{0:T(128)S(1)} all-reduce(s32[64]{0:T(128)S(1)} %bitcast_dynamic-update-slice_fusion), channel_id=2, replica_groups=mesh['groups'=2,'goal'=16] {'goal'}, use_global_device_ids=true, to_apply=%add | all-reduce | flops 64 | bytes 512 | tf_op jit(solution)/shard_map/all_gather | solution.py:57
  146.0 6.9 %copy.24 = bf16[4,64,4096]{1,0,2:T(4,128)(2,1)} copy(bf16[4,64,4096]{2,1,0:T(8,128)(2,1)} %param.8) | data formatting | bytes 4194304 | tf_op args[0]
  152.9 7.6 %reshape.93 = bf16[16,2,32768]{2,1,0:T(2,128)(2,1)} reshape(bf16[4096,4,64]{2,1,0:T(4,128)(2,1)} %bitcast.54) | data formatting | bytes 4194304
  160.5 29.4 %collective-permute-start.5 = (bf16[1,256,256]{2,1,0:T(8,128)(2,1)S(1)}, bf16[1,256,256]{2,1,0:T(8,128)(2,1)S(1)}, u32[]{:S(2)}, u32[]{:S(2)}) collective-permute-start(bf16[1,256,256]{2,1,0:T(8,128)(2,1)S(1)} %get-tuple-element.33), channel_id=1, source_target_pairs={{0,10},{1,11},{2,12},{3,13},{4,14},{5,15},{6,0},{7,1},{8,2},{9,3},... | collective-permute-start | bytes 393224 | tf_op jit(solution)/shard_map/ppermute | solution.py:17
  190.6 10.9 %collective-permute-start.6 = (bf16[1,256,256]{2,1,0:T(8,128)(2,1)}, bf16[1,256,256]{2,1,0:T(8,128)(2,1)S(1)}, u32[]{:S(2)}, u32[]{:S(2)}) collective-permute-start(bf16[1,256,256]{2,1,0:T(8,128)(2,1)} %get-tuple-element.32), channel_id=1, source_target_pairs={{0,9},{1,10},{2,11},{3,12},{4,13},{5,14},{6,15},{7,0},{8,1},{9,2},... | collective-permute-start | bytes 393224 | tf_op jit(solution)/shard_map/ppermute | solution.py:17
  231.7 12.7 %all-to-all-start.1 = ((bf16[16,2,32768]{2,1,0:T(2,128)(2,1)}), bf16[16,2,32768]{2,1,0:T(2,128)(2,1)}, u32[]{:S(2)}, u32[]{:S(2)}) async-start(bf16[16,2,32768]{2,1,0:T(2,128)(2,1)} %reshape.93), calls=%async_computation.1 | async-start | bytes 4194304 | tf_op jit(solution)/shard_map/all_to_all | solution.py:62
  260.3 5.5 %gather_fusion.1 = bf16[64,256,256]{2,1,0:T(8,128)(2,1)} fusion(bf16[16,256,256]{2,1,0:T(8,128)(2,1)S(1)} %constant_dynamic-slice_fusion, s32[1024]{0:T(1024)S(1)} %pad_clamp_fusion), kind=kCustom, calls=%fused_computation.1.clone | custom fusion | bytes 16777472 | tf_op jit(solution)/shard_map/while/body/eval_jaxpr/jit(_take)/gather | solution.py:27
  265.9 10.5 %reshape.92 = bf16[4096,1,256]{2,1,0:T(2,128)(2,1)} reshape(bf16[16,2,32768]{2,1,0:T(2,128)(2,1)} %all-to-all-done) | data formatting | bytes 4194304
  283.1 5.5 %gather_fusion = bf16[64,256,256]{2,1,0:T(8,128)(2,1)} fusion(bf16[16,256,256]{2,1,0:T(8,128)(2,1)S(1)} %bitcast.50, s32[1024]{0:T(1024)S(1)} %pad_clamp_fusion), kind=kCustom, calls=%fused_computation.clone | custom fusion | bytes 16777472 | tf_op jit(solution)/shard_map/while/body/eval_jaxpr/jit(_take)/gather | solution.py:28
  288.6 11.6 %broadcast_select_fusion = (bf16[64,256,256]{2,1,0:T(8,128)(2,1)}, bf16[64,256,256]{2,1,0:T(8,128)(2,1)}) fusion(bf16[64,256,256]{2,1,0:T(8,128)(2,1)} %gather_fusion.1, pred[64]{0:T(512)(128)(4,1)S(1)} %compare_and_fusion, bf16[64,256,256]{2,1,0:T(8,128)(2,1)} %gather_fusion), kind=kLoop, calls=%fused_computation.9 | loop fusion | flops 8388608 | bytes 33554496 | tf_op jit(solution)/shard_map/while/body/eval_jaxpr/jit(_take)/select_n | solution.py:27
  300.2 12.0 %copy.23 = bf16[64,256,256]{1,2,0:T(8,128)(2,1)} copy(bf16[64,256,256]{2,1,0:T(8,128)(2,1)} %get-tuple-element.39) | data formatting | bytes 16777216 | tf_op jit(solution)/shard_map/while/body/eval_jaxpr/jit(_take)/select_n | solution.py:27
  312.2 7.4 %reshape.94 = bf16[4096,4,64]{2,1,0:T(4,128)(2,1)} reshape(bf16[16,2,32768]{2,1,0:T(2,128)(2,1)} %all-to-all-done.1) | data formatting | bytes 4194304
  319.6 5.4 %copy.25 = bf16[4,64,16,256]{3,1,0,2:T(8,128)(2,1)S(1)} copy(bf16[4,64,16,256]{1,0,3,2:T(4,128)(2,1)} %bitcast.53) | data formatting | bytes 4194304 | tf_op jit(solution)/shard_map/all_to_all | solution.py:62
  328.2 11.9 %copy.22 = bf16[64,256,256]{1,2,0:T(8,128)(2,1)} copy(bf16[64,256,256]{2,1,0:T(8,128)(2,1)} %get-tuple-element.40) | data formatting | bytes 16777216 | tf_op jit(solution)/shard_map/while/body/eval_jaxpr/jit(_take)/select_n | solution.py:28
  340.2 12.7 %fusion.6 = f32[64,4,256,64]{2,3,1,0:T(8,128)} fusion(bf16[64,256,4,64]{1,3,2,0:T(8,128)(2,1)} %bitcast.49, bf16[64,64,4,64]{3,2,1,0:T(4,128)(2,1)} %reshape.60), kind=kOutput, calls=%fused_computation.13 | convolution fusion | flops 536870912 | bytes 27262976 | tf_op jit(solution)/shard_map/while/body/eval_jaxpr/tihd,tjhd->thij/dot_general | solution.py:30
  352.9 14.8 %fusion.20 = f32[64,4,64]{2,1,0:T(4,128)S(1)} fusion(f32[64,4,256,64]{2,3,1,0:T(8,128)} %fusion.6), kind=kOutput, calls=%fused_computation.62 | output fusion | flops 8388863 | bytes 16842752 | tf_op jit(solution)/shard_map/while/body/eval_jaxpr/sub | solution.py:34
  367.7 43.3 %fusion.8 = bf16[64,4,64,64]{3,2,1,0:T(8,128)(2,1)} fusion(bf16[64,256,4,64]{1,3,2,0:T(8,128)(2,1)} %bitcast.57, f32[64,4,64]{2,1,0:T(4,128)S(1)} %fusion.20, f32[64,4,256,64]{2,3,1,0:T(8,128)} %fusion.6), kind=kOutput, calls=%fused_computation.15 | convolution fusion | flops 550519040 | bytes 27328512 | tf_op jit(solution)/shard_map/while/body/eval_jaxpr/thij,tjhd->tihd/dot_general | solution.py:36
  411.0 4.8 copy.27
  415.8 6.1 %all-to-all-start.2 = ((bf16[64,64,256]{2,1,0:T(8,128)(2,1)}), bf16[64,64,256]{2,1,0:T(8,128)(2,1)S(1)}, u32[]{:S(2)}, u32[]{:S(2)}) async-start(bf16[64,64,256]{2,1,0:T(8,128)(2,1)} %copy.27), calls=%async_computation.2 | async-start | bytes 4194304 | tf_op jit(solution)/shard_map/all_to_all | solution.py:64
  422.1 47.3 %all-to-all-done.2 = bf16[64,64,256]{2,1,0:T(8,128)(2,1)S(1)} async-done(((bf16[64,64,256]{2,1,0:T(8,128)(2,1)}), bf16[64,64,256]{2,1,0:T(8,128)(2,1)S(1)}, u32[]{:S(2)}, u32[]{:S(2)}) %all-to-all-start.2) | async-done | bytes 2097184 | tf_op jit(solution)/shard_map/all_to_all | solution.py:64
  471.5 9.3 %convolution_convert_fusion = bf16[256,2048]{1,0:T(8,128)(2,1)} fusion(bf16[4096,2048]{1,0:T(8,128)(2,1)} %all-gather.3.cloned.1.call-done, bf16[256,4096]{1,0:T(8,128)(2,1)S(1)} %bitcast.61, pred[256]{0:T(512)(128)(4,1)S(1)} %lt.52), kind=kOutput, calls=%fused_computation.16 | convolution fusion | flops 4296540160 | bytes 19923200 | tf_op jit(solution)/shard_map/dot_general | solution.py:70
  (97 shorter events, 72.0 us)
Async XLA Ops:
  6.5 464.9 %all-gather.3.cloned.1.call-start = ((), (), s32[]{:S(2)}) async-start(), calls=%async_computation.3 | async-start | bytes 17825792 | tf_op jit(solution)/shard_map/all_gather | solution.py:72
  41.5 190.1 %all-to-all-start = ((bf16[16,2,32768]{2,1,0:T(2,128)(2,1)}), bf16[16,2,32768]{2,1,0:T(2,128)(2,1)}, u32[]{:S(2)}, u32[]{:S(2)}) async-start(bf16[16,2,32768]{2,1,0:T(2,128)(2,1)} %reshape.91), calls=%async_computation | async-start | bytes 4194304 | tf_op jit(solution)/shard_map/all_to_all | solution.py:60
  48.1 9.0 %copy-start.6 = (u32[32]{0:T(128)S(1)}, u32[32]{0:T(128)}, u32[]{:S(2)}) copy-start(u32[32]{0:T(128)} %constant.86) | copy-start | bytes 388
  48.1 10.1 %copy-start.4 = (s32[4,1]{0,1:T(1,128)S(1)}, s32[4,1]{0,1:T(1,128)}, u32[]{:S(2)}) copy-start(s32[4,1]{0,1:T(1,128)} %param.12) | copy-start | bytes 52
  51.5 109.0 %collective-permute-start = (bf16[1,256,256]{2,1,0:T(8,128)(2,1)S(1)}, bf16[1,256,256]{2,1,0:T(8,128)(2,1)S(1)}, u32[]{:S(2)}, u32[]{:S(2)}) collective-permute-start(bf16[1,256,256]{2,1,0:T(8,128)(2,1)S(1)} %get-tuple-element.38), channel_id=1, source_target_pairs={{0,15},{1,0},{2,1},{3,2},{4,3},{5,4},{6,5},{7,6},{8,7},{9,8},{10,9... | collective-permute-start | bytes 393224 | tf_op jit(solution)/shard_map/ppermute | solution.py:17
  51.8 138.8 %collective-permute-start.1 = (bf16[1,256,256]{2,1,0:T(8,128)(2,1)S(1)}, bf16[1,256,256]{2,1,0:T(8,128)(2,1)S(1)}, u32[]{:S(2)}, u32[]{:S(2)}) collective-permute-start(bf16[1,256,256]{2,1,0:T(8,128)(2,1)S(1)} %get-tuple-element.37), channel_id=1, source_target_pairs={{0,14},{1,15},{2,0},{3,1},{4,2},{5,3},{6,4},{7,5},{8,6},{9,7},{10,... | collective-permute-start | bytes 393224 | tf_op jit(solution)/shard_map/ppermute | solution.py:17
  52.1 150.1 %collective-permute-start.2 = (bf16[1,256,256]{2,1,0:T(8,128)(2,1)S(1)}, bf16[1,256,256]{2,1,0:T(8,128)(2,1)S(1)}, u32[]{:S(2)}, u32[]{:S(2)}) collective-permute-start(bf16[1,256,256]{2,1,0:T(8,128)(2,1)S(1)} %get-tuple-element.36), channel_id=1, source_target_pairs={{0,13},{1,14},{2,15},{3,0},{4,1},{5,2},{6,3},{7,4},{8,5},{9,6},{10... | collective-permute-start | bytes 393224 | tf_op jit(solution)/shard_map/ppermute | solution.py:17
  53.6 149.2 %collective-permute-start.3 = (bf16[1,256,256]{2,1,0:T(8,128)(2,1)S(1)}, bf16[1,256,256]{2,1,0:T(8,128)(2,1)S(1)}, u32[]{:S(2)}, u32[]{:S(2)}) collective-permute-start(bf16[1,256,256]{2,1,0:T(8,128)(2,1)S(1)} %get-tuple-element.35), channel_id=1, source_target_pairs={{0,12},{1,13},{2,14},{3,15},{4,0},{5,1},{6,2},{7,3},{8,4},{9,5},{1... | collective-permute-start | bytes 393224 | tf_op jit(solution)/shard_map/ppermute | solution.py:17
  56.8 149.6 %collective-permute-start.4 = (bf16[1,256,256]{2,1,0:T(8,128)(2,1)S(1)}, bf16[1,256,256]{2,1,0:T(8,128)(2,1)S(1)}, u32[]{:S(2)}, u32[]{:S(2)}) collective-permute-start(bf16[1,256,256]{2,1,0:T(8,128)(2,1)S(1)} %get-tuple-element.34), channel_id=1, source_target_pairs={{0,11},{1,12},{2,13},{3,14},{4,15},{5,0},{6,1},{7,2},{8,3},{9,4},{... | collective-permute-start | bytes 393224 | tf_op jit(solution)/shard_map/ppermute | solution.py:17
  160.5 47.2 %collective-permute-start.5 = (bf16[1,256,256]{2,1,0:T(8,128)(2,1)S(1)}, bf16[1,256,256]{2,1,0:T(8,128)(2,1)S(1)}, u32[]{:S(2)}, u32[]{:S(2)}) collective-permute-start(bf16[1,256,256]{2,1,0:T(8,128)(2,1)S(1)} %get-tuple-element.33), channel_id=1, source_target_pairs={{0,10},{1,11},{2,12},{3,13},{4,14},{5,15},{6,0},{7,1},{8,2},{9,3},... | collective-permute-start | bytes 393224 | tf_op jit(solution)/shard_map/ppermute | solution.py:17
  190.6 17.8 %collective-permute-start.6 = (bf16[1,256,256]{2,1,0:T(8,128)(2,1)}, bf16[1,256,256]{2,1,0:T(8,128)(2,1)S(1)}, u32[]{:S(2)}, u32[]{:S(2)}) collective-permute-start(bf16[1,256,256]{2,1,0:T(8,128)(2,1)} %get-tuple-element.32), channel_id=1, source_target_pairs={{0,9},{1,10},{2,11},{3,12},{4,13},{5,14},{6,15},{7,0},{8,1},{9,2},... | collective-permute-start | bytes 393224 | tf_op jit(solution)/shard_map/ppermute | solution.py:17
  202.2 11.0 %collective-permute-start.7 = (bf16[1,256,256]{2,1,0:T(8,128)(2,1)}, bf16[1,256,256]{2,1,0:T(8,128)(2,1)S(1)}, u32[]{:S(2)}, u32[]{:S(2)}) collective-permute-start(bf16[1,256,256]{2,1,0:T(8,128)(2,1)} %get-tuple-element.31), channel_id=1, source_target_pairs={{0,8},{1,9},{2,10},{3,11},{4,12},{5,13},{6,14},{7,15},{8,0},{9,1},... | collective-permute-start | bytes 393224 | tf_op jit(solution)/shard_map/ppermute | solution.py:17
  202.8 11.0 %collective-permute-start.8 = (bf16[1,256,256]{2,1,0:T(8,128)(2,1)}, bf16[1,256,256]{2,1,0:T(8,128)(2,1)S(1)}, u32[]{:S(2)}, u32[]{:S(2)}) collective-permute-start(bf16[1,256,256]{2,1,0:T(8,128)(2,1)} %get-tuple-element.30), channel_id=1, source_target_pairs={{0,7},{1,8},{2,9},{3,10},{4,11},{5,12},{6,13},{7,14},{8,15},{9,0},... | collective-permute-start | bytes 393224 | tf_op jit(solution)/shard_map/ppermute | solution.py:17
  206.4 10.0 %collective-permute-start.9 = (bf16[1,256,256]{2,1,0:T(8,128)(2,1)}, bf16[1,256,256]{2,1,0:T(8,128)(2,1)S(1)}, u32[]{:S(2)}, u32[]{:S(2)}) collective-permute-start(bf16[1,256,256]{2,1,0:T(8,128)(2,1)} %get-tuple-element.29), channel_id=1, source_target_pairs={{0,6},{1,7},{2,8},{3,9},{4,10},{5,11},{6,12},{7,13},{8,14},{9,15},... | collective-permute-start | bytes 393224 | tf_op jit(solution)/shard_map/ppermute | solution.py:17
  207.7 11.6 %collective-permute-start.10 = (bf16[1,256,256]{2,1,0:T(8,128)(2,1)}, bf16[1,256,256]{2,1,0:T(8,128)(2,1)S(1)}, u32[]{:S(2)}, u32[]{:S(2)}) collective-permute-start(bf16[1,256,256]{2,1,0:T(8,128)(2,1)} %get-tuple-element.28), channel_id=1, source_target_pairs={{0,5},{1,6},{2,7},{3,8},{4,9},{5,10},{6,11},{7,12},{8,13},{9,14},{... | collective-permute-start | bytes 393224 | tf_op jit(solution)/shard_map/ppermute | solution.py:17
  208.4 13.7 %collective-permute-start.11 = (bf16[1,256,256]{2,1,0:T(8,128)(2,1)}, bf16[1,256,256]{2,1,0:T(8,128)(2,1)S(1)}, u32[]{:S(2)}, u32[]{:S(2)}) collective-permute-start(bf16[1,256,256]{2,1,0:T(8,128)(2,1)} %get-tuple-element.26), channel_id=1, source_target_pairs={{0,4},{1,5},{2,6},{3,7},{4,8},{5,9},{6,10},{7,11},{8,12},{9,13},{1... | collective-permute-start | bytes 393224 | tf_op jit(solution)/shard_map/ppermute | solution.py:17
  213.1 11.8 %collective-permute-start.12 = (bf16[1,256,256]{2,1,0:T(8,128)(2,1)}, bf16[1,256,256]{2,1,0:T(8,128)(2,1)S(1)}, u32[]{:S(2)}, u32[]{:S(2)}) collective-permute-start(bf16[1,256,256]{2,1,0:T(8,128)(2,1)} %get-tuple-element.24), channel_id=1, source_target_pairs={{0,3},{1,4},{2,5},{3,6},{4,7},{5,8},{6,9},{7,10},{8,11},{9,12},{10... | collective-permute-start | bytes 393224 | tf_op jit(solution)/shard_map/ppermute | solution.py:17
  213.8 13.9 %collective-permute-start.13 = (bf16[1,256,256]{2,1,0:T(8,128)(2,1)}, bf16[1,256,256]{2,1,0:T(8,128)(2,1)S(1)}, u32[]{:S(2)}, u32[]{:S(2)}) collective-permute-start(bf16[1,256,256]{2,1,0:T(8,128)(2,1)} %get-tuple-element.17), channel_id=1, source_target_pairs={{0,2},{1,3},{2,4},{3,5},{4,6},{5,7},{6,8},{7,9},{8,10},{9,11},{10,... | collective-permute-start | bytes 393224 | tf_op jit(solution)/shard_map/ppermute | solution.py:17
  216.4 13.2 %collective-permute-start.14 = (bf16[1,256,256]{2,1,0:T(8,128)(2,1)}, bf16[1,256,256]{2,1,0:T(8,128)(2,1)S(1)}, u32[]{:S(2)}, u32[]{:S(2)}) collective-permute-start(bf16[1,256,256]{2,1,0:T(8,128)(2,1)} %get-tuple-element.16), channel_id=1, source_target_pairs={{0,1},{1,2},{2,3},{3,4},{4,5},{5,6},{6,7},{7,8},{8,9},{9,10},{10,1... | collective-permute-start | bytes 393224 | tf_op jit(solution)/shard_map/ppermute | solution.py:17
  224.9 0.7 copy-start.1
  229.7 0.7 copy-start.3
  231.7 80.5 %all-to-all-start.1 = ((bf16[16,2,32768]{2,1,0:T(2,128)(2,1)}), bf16[16,2,32768]{2,1,0:T(2,128)(2,1)}, u32[]{:S(2)}, u32[]{:S(2)}) async-start(bf16[16,2,32768]{2,1,0:T(2,128)(2,1)} %reshape.93), calls=%async_computation.1 | async-start | bytes 4194304 | tf_op jit(solution)/shard_map/all_to_all | solution.py:62
  411.0 10.9 %copy-start.5 = (s32[4]{0:T(128)S(1)}, s32[4]{0:T(128)}, u32[]{:S(2)}) copy-start(s32[4]{0:T(128)} %param.13) | copy-start | bytes 52
  415.8 53.5 %all-to-all-start.2 = ((bf16[64,64,256]{2,1,0:T(8,128)(2,1)}), bf16[64,64,256]{2,1,0:T(8,128)(2,1)S(1)}, u32[]{:S(2)}, u32[]{:S(2)}) async-start(bf16[64,64,256]{2,1,0:T(8,128)(2,1)} %copy.27), calls=%async_computation.2 | async-start | bytes 4194304 | tf_op jit(solution)/shard_map/all_to_all | solution.py:64
  (2 other events, 1.3 us)
Sparse Core Ops, SparseCore 0:
  9.5 166.1 all-gather.2
